TPU v7x, 128 devices: a whole 4x4x4 slice. The times are simulated.
128 devices in a mesh: sub: 32 (over y_hi, x, z), freq: 4 (over y_lo, core).
Axes of the slice: x: 4, y: 4 (y_hi: 2, y_lo: 2; y = y_hi * 2 + y_lo), z: 4, core: 2. Of those that a mesh axis runs over, the one named last changes fastest.
Arguments:
- z_vectors: bfloat16 [1572864, 64], P(('freq', 'sub')), parts along dimension 0, may hold values from -0.0546875 to 0.0546875
- band_tiles: bfloat16 [8, 3072, 3, 128, 128], P('freq', 'sub'), parts along dimension 0, may hold values from -6 to 6
- coupling_tiles: bfloat16 [8, 192, 512, 512], P('freq', 'sub'), parts along dimension 0, may hold values from -24 to 24
- neighbours: int32 [32, 6], P('sub'), may hold values from 0 to 31, as said below
- interface_rows: int32 [32, 6, 512], P('sub'), may hold values from 0 to 12287
- coarse_number: int32 [32], replicated, may hold values from 0 to 31, each once
Outputs:
- coarse: float32 [8, 2048, 2048], P('freq', 'sub'), parts along dimension 0
There are 4 independent parts, one for each index of `freq`. A program takes and returns all parts, laid end to end along the dimension named above; an argument that names none is the same for every part. Nothing has to cross between parts.
Inputs may be any that keep to these rules, and one draw needn't show every extreme that they name: The neighbours of a subdomain are 6 distinct subdomains other than itself, and if t is in slot j of s then s is in slot 5 - j of t.
All inputs are finite; a program needn't handle non-finite values.
Results may differ from a plain program's by a relative error of at most 0.0029.
Values may be sent and summed in bfloat16 or wider, within the bound.
No kernel may reach another device: no remote copies, remote signals or barrier semaphores. Data moves between devices by JAX's collectives and lax.ppermute only.
A program may use at most 128 MiB of HBM per device.

v0:
```python
import jax
import jax.numpy as jnp
from jax import lax
from jax.sharding import PartitionSpec as P


def body(z_vectors, band_tiles, coupling_tiles, neighbours, interface_rows, coarse_number):
    hp = lax.Precision.HIGHEST
    width = z_vectors.shape[1]
    slots = neighbours.shape[1]
    span = interface_rows.shape[2]
    nblocks = band_tiles.shape[1]
    tile_rows = band_tiles.shape[-1]
    sub_count = lax.axis_size("sub")
    myself = lax.axis_index("sub")
    nbrs = neighbours[0]
    own_rows = interface_rows[0]
    subjects = jnp.arange(sub_count, dtype=jnp.int32)
    local_rows = z_vectors[own_rows.reshape(-1)].reshape(slots, span * width)
    picker = nbrs[:, None] == subjects[None, :]
    picker_half = picker.astype(jnp.bfloat16)
    gathered = lax.all_gather(local_rows[::-1][None], "sub", axis=0, tiled=True)
    remote = jnp.einsum(
        "js,sjx->jx", picker_half, gathered, preferred_element_type=jnp.float32
    ).astype(jnp.bfloat16)
    zblocks = z_vectors.reshape(nblocks, tile_rows, width)
    zpad = jnp.pad(zblocks, ((1, 1), (0, 0), (0, 0)))
    zshift = jnp.stack([zpad[0:nblocks], zpad[1 : nblocks + 1], zpad[2 : nblocks + 2]], axis=1)
    image = jnp.einsum(
        "rbkij,bkjn->rbin", band_tiles, zshift, preferred_element_type=jnp.float32
    ).astype(jnp.bfloat16)
    diag_block = jnp.einsum("bin,rbim->rnm", zblocks, image, preferred_element_type=jnp.float32)
    cross = jnp.einsum(
        "rjab,jbn->rjan",
        coupling_tiles,
        remote.reshape(slots, span, width),
        preferred_element_type=jnp.float32,
    ).astype(jnp.bfloat16)
    off_block = jnp.einsum(
        "jan,rjam->rjnm",
        local_rows.reshape(slots, span, width),
        cross,
        preferred_element_type=jnp.float32,
    )
    blocks = jnp.concatenate([diag_block[:, None], off_block], axis=1)
    nbr_cols = jnp.sum(picker.astype(jnp.int32) * coarse_number[None, :], axis=1)
    own_col = jnp.sum(jnp.where(subjects == myself, coarse_number, 0))
    cols = jnp.concatenate([own_col[None], nbr_cols])
    onehot = (cols[:, None] == subjects[None, :]).astype(jnp.float32)
    row = jnp.einsum("js,rjnm->rnsm", onehot, blocks, precision=hp)
    return row.reshape(2, width, sub_count * width)


def solution(mesh):
    in_specs = (
        P(("freq", "sub"), None),
        P("freq", "sub", None, None, None),
        P("freq", "sub", None, None),
        P("sub", None),
        P("sub", None, None),
        P(),
    )
    out_specs = P("freq", "sub", None)
    return jax.shard_map(body, mesh=mesh, in_specs=in_specs, out_specs=out_specs, check_vma=False)
```

profile of v0, /device:TPU:1, one launch (start us, length us, event | category | flops | bytes accessed | tf_op | source)
XLA Modules:
  0.0 293.6 jit_solution(16182070276823379440)
XLA Ops:
  6.5 0.0 copy-start.2
  6.5 0.0 all-gather.4.cloned.1.call-start
  6.5 3.1 %copy.32 = bf16[12288,64]{1,0:T(8,128)(2,1)S(1)} copy(bf16[12288,64]{0,1:T(8,128)(2,1)} %param.6) | data formatting | bytes 3145728 | tf_op args[0]
  9.6 0.0 copy-done.2
  9.7 11.5 %gather_fusion = bf16[3072,64]{1,0:T(8,128)(2,1)} fusion(bf16[12288,64]{1,0:T(8,128)(2,1)S(1)} %copy.32, s32[3072]{0:T(1024)S(1)} %broadcast_clamp_fusion), kind=kCustom, calls=%fused_computation | custom fusion | bytes 798720 | tf_op jit(solution)/shard_map/gather | solution.py:19
  21.2 0.0 copy-start
  21.2 1.9 reshape.45
  23.1 76.5 %rev.3 = bf16[6,32768]{1,0:T(8,128)(2,1)} reverse(bf16[6,32768]{1,0:T(8,128)(2,1)S(1)} %reshape.45), dimensions={0} | reverse | bytes 786432 | tf_op jit(solution)/shard_map/rev | solution.py:22
  99.6 0.0 all-gather.4.cloned.1.call-update
  99.6 0.0 copy-done
  99.6 0.3 copy.50
  99.9 0.0 copy-start.3
  99.9 0.0 copy-start.4
  99.9 0.6 copy.30
  100.6 0.0 copy-done.3
  100.6 0.6 fusion.33
  101.2 0.0 copy-done.4
  101.2 0.2 select_reduce_fusion
  101.4 0.7 pad_add_fusion
  102.1 0.4 copy_bitcast_fusion
  102.5 2.4 slice_bitcast_fusion.1
  105.0 0.1 fusion.29
  105.1 11.5 %fusion.21 = f32[2,1,64,64]{2,3,0,1:T(8,128)S(1)} fusion(bf16[2,96,3,128,128]{4,3,2,1,0:T(8,128)(2,1)} %param.7, bf16[96,1,128,64]{2,3,1,0:T(8,128)(2,1)} %get-tuple-element.6, bf16[96,1,128,64]{2,3,1,0:T(8,128)(2,1)S(1)} %copy.30, bf16[96,1,128,64]{2,3,1,0:T(8,128)(2,1)} %get-tuple-element.5, bf16[12288,64]{0,1:T(8,128)(2,1)S(1)} %copy-done), kind=kOutput, calls=%fused_computation.22 | convolution fusion | flops 1425014784 | bytes 25198592 | tf_op jit(solution)/shard_map/bin,rbim->rnm/dot_general | solution.py:32
  116.5 141.2 %all-gather.4.cloned.1.call-done = bf16[32,6,32768]{2,1,0:T(8,128)(2,1)} async-done(((bf16[1,6,32768]{2,1,0:T(8,128)(2,1)}), bf16[32,6,32768]{2,1,0:T(8,128)(2,1)}) %all-gather.4.cloned.1.call-update) | async-done | bytes 12582928 | tf_op jit(solution)/shard_map/all_gather | solution.py:22
  257.8 19.6 %fusion = bf16[6,1,32768]{2,1,0:T(2,128)(2,1)S(1)} fusion(bf16[32,6,32768]{2,1,0:T(8,128)(2,1)} %all-gather.4.cloned.1.call-done, pred[6,32,1]{1,0,2:T(8,128)(4,1)S(1)} %fusion.29), kind=kOutput, calls=%fused_computation.1 | convolution fusion | flops 12582912 | bytes 12976320 | tf_op jit(solution)/shard_map/js,sjx->jx/dot_general | solution.py:23
  277.4 0.0 copy-start.1
  277.4 0.4 copy.68
  277.8 0.8 reshape.46
  278.7 0.0 copy-done.1
  278.7 5.0 %convolution_bitcast_fusion.1 = f32[2,6,64,64]{2,3,0,1:T(8,128)S(1)} fusion(bf16[6,512,64,1]{2,1,3,0:T(8,128)(2,1)S(1)} %bitcast.97, bf16[2,6,512,512]{3,2,1,0:T(8,128)(2,1)} %param.8, bf16[6,512,64]{2,1,0:T(8,128)(2,1)S(1)} %reshape.46), kind=kOutput, calls=%fused_computation.21 | convolution fusion | flops 453378048 | bytes 7274496 | tf_op jit(solution)/shard_map/jan,rjam->rjnm/dot_general | solution.py:39
  283.8 0.2 copy.36
  284.0 1.1 convolution_bitcast_fusion
  285.1 1.6 reshape.47
  (3 shorter events, 0.1 us)
Async XLA Ops:
  6.5 3.1 %copy-start.2 = (s32[1,6,512]{2,0,1:T(1,128)S(1)}, s32[1,6,512]{2,0,1:T(1,128)}, u32[]{:S(2)}) copy-start(s32[1,6,512]{2,0,1:T(1,128)} %param.10) | copy-start | bytes 36868
  6.5 251.2 %all-gather.4.cloned.1.call-start = ((), (), s32[]{:S(2)}) async-start(), calls=%async_computation | async-start | bytes 17301504 | tf_op jit(solution)/shard_map/all_gather | solution.py:22
  21.2 78.4 %copy-start = (bf16[12288,64]{0,1:T(8,128)(2,1)S(1)}, bf16[12288,64]{0,1:T(8,128)(2,1)}, u32[]{:S(2)}) copy-start(bf16[12288,64]{0,1:T(8,128)(2,1)} %param.6) | copy-start | bytes 4718596
  99.9 0.7 copy-start.3
  99.9 1.3 copy-start.4
  277.4 1.3 copy-start.1
Sparse Core Ops, SparseCore 0:
  99.7 157.9 all-gather.3
where the time goes:
time: 294 us
  waiting for transfers between devices  141 us (48%)
  local copies, waits for them, and re-layouts  99.9 us (34%)
  matrix products  37.2 us (13%)
  between operations  13.5 us (5%)
    all_gather x1, waiting for transfers between devices, body(): gathered = lax.all_gather(local_rows[::-1][None], 'sub', axis=0, tiled=True)  141 us
    rev x1, local copies, waits for them, and re-layouts, body(): gathered = lax.all_gather(local_rows[::-1][None], 'sub', axis=0, tiled=True)  76.5 us
    dot_general x1, matrix products, body(): jnp.einsum('js,sjx->jx', picker_half, gathered, preferred_element_type=jn...  19.6 us
    gather x1, local copies, waits for them, and re-layouts, body(): local_rows = z_vectors[own_rows.reshape(-1)].reshape(slots, span * width)  11.5 us
    dot_general x1, matrix products, body(): jnp.einsum('bin,rbim->rnm', zblocks, image, preferred_element_type=jnp.fl...  11.5 us
  transfers between devices with their start and end apart: 1, of which 1 were waited for; matrix products, arithmetic and copies ran while one was open for 6% of the time, Pallas kernels for 0%

commit v1 on v0

v1 whole, which is shorter than its diff:
```python
import functools

import jax
import jax.numpy as jnp
from jax import lax
from jax.experimental import pallas as pl
from jax.experimental.pallas import tpu as pltpu
from jax.sharding import PartitionSpec as P

GROUP = 1024


def gather_kernel(nbr_ref, rows_ref, z_ref, send_ref, local_ref, stack, sems):
    width, count = z_ref.shape
    slots, _, span = rows_ref.shape
    groups = count // GROUP
    for g in range(groups):
        stack[g * width : (g + 1) * width, :] = z_ref[:, g * GROUP : (g + 1) * GROUP]
    local_iota = lax.broadcasted_iota(jnp.int32, (GROUP, span), 0)

    def step(j, carry):
        rows = rows_ref[j]
        low = rows % GROUP
        group = rows // GROUP
        onehot = jnp.where(local_iota == low, 1.0, 0.0).astype(jnp.bfloat16)
        found = jnp.dot(stack[...], onehot, preferred_element_type=jnp.float32)
        picked = found[0:width]
        for g in range(1, groups):
            picked = jnp.where(group == g, found[g * width : (g + 1) * width], picked)
        local_ref[j] = picked.astype(jnp.bfloat16)
        pltpu.make_async_copy(local_ref.at[j], send_ref.at[nbr_ref[j]], sems.at[j]).start()
        return carry

    lax.fori_loop(0, slots, step, 0)
    for j in range(slots):
        pltpu.make_async_copy(local_ref.at[j], send_ref.at[nbr_ref[j]], sems.at[j]).wait()


def final_kernel(nbr_ref, col_ref, me_ref, recv_ref, y_ref, diag_ref, out_ref, held, sems):
    slots, _, span = y_ref.shape
    width = diag_ref.shape[1]

    def fetch(j):
        return pltpu.make_async_copy(recv_ref.at[nbr_ref[j]], held.at[j], sems.at[j])

    for j in range(slots):
        fetch(j).start()
    out_ref[...] = jnp.zeros_like(out_ref)
    upper = lax.broadcasted_iota(jnp.int32, (width, 2 * width), 1) // width

    def place(r, col, value):
        where = pl.ds(pl.multiple_of((col // 2) * 2 * width, 2 * width), 2 * width)
        out_ref[r, :, where] += jnp.where(upper == col % 2, value, 0.0)

    own = col_ref[me_ref[0]]
    for r in range(2):
        value = diag_ref[r]
        place(r, own, jnp.concatenate([value, value], axis=1))
    for j in range(slots):
        fetch(j).wait()
        far = held[j]
        both = lax.dot_general(
            y_ref[j],
            jnp.concatenate([far, far], axis=0),
            (((1,), (1,)), ((), ())),
            preferred_element_type=jnp.float32,
        )
        col = col_ref[nbr_ref[j]]
        for r in range(2):
            high = both[2 * r * width : (2 * r + 1) * width]
            low = both[(2 * r + 1) * width : (2 * r + 2) * width]
            place(r, col, high + low)


def body(z_vectors, band_tiles, coupling_tiles, neighbours, interface_rows, coarse_number):
    count, width = z_vectors.shape
    slots = neighbours.shape[1]
    span = interface_rows.shape[2]
    nblocks = band_tiles.shape[1]
    tile_rows = band_tiles.shape[-1]
    sub_count = lax.axis_size("sub")
    myself = lax.axis_index("sub")
    nbrs = neighbours[0]
    smem = pl.BlockSpec(memory_space=pltpu.SMEM)
    vmem = pl.BlockSpec(memory_space=pltpu.VMEM)
    anywhere = pl.BlockSpec(memory_space=pl.ANY)
    send, local = pl.pallas_call(
        gather_kernel,
        out_shape=(
            jax.ShapeDtypeStruct((sub_count, width, span), jnp.bfloat16),
            jax.ShapeDtypeStruct((slots, width, span), jnp.bfloat16),
        ),
        in_specs=[smem, vmem, vmem],
        out_specs=(anywhere, vmem),
        scratch_shapes=[
            pltpu.VMEM((count // GROUP * width, GROUP), jnp.bfloat16),
            pltpu.SemaphoreType.DMA((slots,)),
        ],
        compiler_params=pltpu.CompilerParams(vmem_limit_bytes=32 * 1024 * 1024),
    )(nbrs, interface_rows[0][:, None, :], z_vectors.T)
    recv = lax.all_to_all(send, "sub", 0, 0, tiled=True)

    zblocks = z_vectors.reshape(nblocks, tile_rows, width)
    zpad = jnp.pad(zblocks, ((1, 1), (0, 0), (0, 0)))
    zshift = jnp.stack([zpad[0:nblocks], zpad[1 : nblocks + 1], zpad[2 : nblocks + 2]], axis=1)
    image = jnp.einsum(
        "rbkij,bkjn->rbin", band_tiles, zshift, preferred_element_type=jnp.float32
    ).astype(jnp.bfloat16)
    diag_block = jnp.einsum("bin,rbim->rnm", zblocks, image, preferred_element_type=jnp.float32)
    y = jnp.einsum("jna,rjab->jrnb", local, coupling_tiles, preferred_element_type=jnp.float32)
    y_high = lax.reduce_precision(y, 8, 7)
    y_low = (y - y_high).astype(jnp.bfloat16)
    y_high = y_high.astype(jnp.bfloat16)
    y_both = jnp.stack([y_high, y_low], axis=2).reshape(slots, 4 * width, span)

    return pl.pallas_call(
        final_kernel,
        out_shape=jax.ShapeDtypeStruct((2, width, sub_count * width), jnp.float32),
        in_specs=[smem, smem, smem, anywhere, vmem, vmem],
        out_specs=vmem,
        scratch_shapes=[
            pltpu.VMEM((slots, width, span), jnp.bfloat16),
            pltpu.SemaphoreType.DMA((slots,)),
        ],
        compiler_params=pltpu.CompilerParams(vmem_limit_bytes=32 * 1024 * 1024),
    )(nbrs, coarse_number, myself.astype(jnp.int32)[None], recv, y_both, diag_block)


def solution(mesh):
    in_specs = (
        P(("freq", "sub"), None),
        P("freq", "sub", None, None, None),
        P("freq", "sub", None, None),
        P("sub", None),
        P("sub", None, None),
        P(),
    )
    out_specs = P("freq", "sub", None)
    return jax.shard_map(body, mesh=mesh, in_specs=in_specs, out_specs=out_specs, check_vma=False)
```

time: 294 us -> 55.6 us (0.19)
  waiting for transfers between devices: 141 us -> 3.4 us
  local copies, waits for them, and re-layouts: 99.9 us -> 9.26 us
  matrix products: 37.2 us -> 16.3 us
  between operations: 13.5 us -> 0.07 us
  starting transfers between devices: 0.01 us -> 11.5 us
  Pallas kernels: 0 us -> 11.4 us
    all_gather x1 -> x0, waiting for transfers between devices: 141 us -> none  [body(): gathered = lax.all_gather(local_rows[::-1][None], 'sub', axis=0, tiled=True)]
    rev x1 -> x0, local copies, waits for them, and re-layouts: 76.5 us -> none  [body(): gathered = lax.all_gather(local_rows[::-1][None], 'sub', axis=0, tiled=True)]
    dot_general x3 -> x1, matrix products: 25.7 us -> 3.95 us  [body(): jnp.einsum('jna,rjab->jrnb', local, coupling_tiles, preferred_element_typ...]
    gather x1 -> x0, local copies, waits for them, and re-layouts: 11.5 us -> none  [body(): local_rows = z_vectors[own_rows.reshape(-1)].reshape(slots, span * width)]
    all_to_all x0 -> x1, starting transfers between devices: none -> 11.5 us  [body(): recv = lax.all_to_all(send, 'sub', 0, 0, tiled=True)]
    pallas_call x0 -> x2, Pallas kernels: none -> 11.4 us  [the longest x1 7.28 us: body(): pl.pallas_call(gather_kernel, out_shape=(jax.ShapeDtypeStruct((sub_count,...]
    reshape x4 -> x0, local copies, waits for them, and re-layouts: 4.83 us -> none  [the longest x1 1.92 us: body(): local_rows = z_vectors[own_rows.reshape(-1)].reshape(slots, span * width)]
    all_to_all x0 -> x1, waiting for transfers between devices: none -> 3.4 us  [body(): recv = lax.all_to_all(send, 'sub', 0, 0, tiled=True)]
  transfers between devices with their start and end apart: 1 -> 1, of which waited for: 1 -> 1; matrix products, arithmetic and copies ran while one was open for 6% -> 44% of each run, Pallas kernels for 0% -> 0%
where the time goes in v1:
time: 55.6 us; the launch traced here: 54.5 us
  matrix products  16.3 us (29%)
  starting transfers between devices  11.5 us (21%)
  Pallas kernels  11.4 us (21%)
  local copies, waits for them, and re-layouts  9.26 us (17%)
  waiting for transfers between devices  3.4 us (6%)
  other arithmetic  2.57 us (5%)
    dot_general x1, matrix products, body(): jnp.einsum('bin,rbim->rnm', zblocks, image, preferred_element_type=jnp.fl...  12.4 us
    all_to_all x1, starting transfers between devices, body(): recv = lax.all_to_all(send, 'sub', 0, 0, tiled=True)  11.5 us
    pallas_call x1, Pallas kernels, body(): pl.pallas_call(gather_kernel, out_shape=(jax.ShapeDtypeStruct((sub_count,...  7.28 us
    unnamed x15, local copies, waits for them, and re-layouts  5.53 us
    pallas_call x1, Pallas kernels, body(): pl.pallas_call(final_kernel, out_shape=jax.ShapeDtypeStruct((2, width, su...  4.11 us
    dot_general x1, matrix products, body(): jnp.einsum('jna,rjab->jrnb', local, coupling_tiles, preferred_element_typ...  3.95 us
    another operation x1, local copies, waits for them, and re-layouts, body(): jnp.stack([zpad[0:nblocks], zpad[1:nblocks + 1], zpad[2:nblocks + 2]], ax...  3.62 us
    all_to_all x1, waiting for transfers between devices, body(): recv = lax.all_to_all(send, 'sub', 0, 0, tiled=True)  3.4 us
  transfers between devices with their start and end apart: 1, of which 1 were waited for; matrix products, arithmetic and copies ran while one was open for 44% of the time, Pallas kernels for 0%

profile of v1, /device:TPU:1, one launch (start us, length us, event | category | flops | bytes accessed | tf_op | source)
XLA Modules:
  0.0 54.5 jit_solution(1975340392325828276)
XLA Ops:
  0.0 0.0 copy-start
  0.0 1.4 %copy-done = bf16[12288,64]{0,1:T(8,128)(2,1)S(1)} copy-done((bf16[12288,64]{0,1:T(8,128)(2,1)S(1)}, bf16[12288,64]{0,1:T(8,128)(2,1)}, u32[]{:S(2)}) %copy-start) | copy-done | bytes 1572888
  1.4 0.0 copy-start.2
  1.4 0.7 %copy-done.2 = s32[1,6,512]{2,0,1:T(1,128)S(1)} copy-done((s32[1,6,512]{2,0,1:T(1,128)S(1)}, s32[1,6,512]{2,0,1:T(1,128)}, u32[]{:S(2)}) %copy-start.2) | copy-done | bytes 12312
  2.1 0.0 copy-start.3
  2.1 0.7 %copy-done.3 = s32[1,6]{1,0:T(1,128)S(1)} copy-done((s32[1,6]{1,0:T(1,128)S(1)}, s32[1,6]{1,0:T(1,128)}, u32[]{:S(2)}) %copy-start.3) | copy-done | bytes 48
  2.8 7.3 %shard_map.64 = (bf16[32,64,512]{2,1,0:T(8,128)(2,1)}, bf16[6,64,512]{2,1,0:T(8,128)(2,1)S(1)}) custom-call(s32[6]{0:T(128)S(1)} %bitcast.74, s32[6,1,512]{2,1,0:T(1,128)S(1)} %bitcast.73, bf16[64,12288]{1,0:T(8,128)(2,1)S(1)} %bitcast.70), custom_call_target="tpu_custom_call" | custom-call | tf_op jit(solution)/shard_map/pallas_call | solution.py:87
  10.1 11.5 %all-to-all-start = ((bf16[32,64,512]{2,1,0:T(8,128)(2,1)}), bf16[32,64,512]{2,1,0:T(8,128)(2,1)}, u32[]{:S(2)}, u32[]{:S(2)}) async-start(bf16[32,64,512]{2,1,0:T(8,128)(2,1)} %get-tuple-element.7), calls=%async_computation | async-start | bytes 4194304 | tf_op jit(solution)/shard_map/all_to_all | solution.py:101
  21.6 4.0 %fusion.19 = (bf16[6,2,1,64,512]{4,3,1,0,2:T(8,128)(2,1)S(1)}, bf16[6,2,1,64,512]{4,3,1,0,2:T(8,128)(2,1)S(1)}) fusion(bf16[2,6,512,512]{3,2,1,0:T(8,128)(2,1)} %param.8, bf16[6,64,512]{2,1,0:T(8,128)(2,1)S(1)} %get-tuple-element.8), kind=kOutput, calls=%fused_computation.18 | convolution fusion | flops 404226048 | bytes 8257536 | tf_op jit(solution)/shard_map/jna,rjab->jrnb/dot_general | solution.py:110
  25.5 0.1 pad_maximum_fusion
  25.7 0.0 copy-start.1
  25.7 0.1 copy.8
  25.8 1.3 %copy-done.1 = bf16[12288,64]{0,1:T(8,128)(2,1)S(1)} copy-done((bf16[12288,64]{0,1:T(8,128)(2,1)S(1)}, bf16[12288,64]{0,1:T(8,128)(2,1)}, u32[]{:S(2)}) %copy-start.1) | copy-done | bytes 1572888
  27.1 1.5 %copy.17 = bf16[8,8,96,128]{3,2,1,0:T(8,128)(2,1)} copy(bf16[8,8,96,128]{3,1,2,0:T(8,128)(2,1)S(1)} %bitcast.71) | data formatting | bytes 3145728
  28.5 0.0 copy-start.6
  28.5 3.6 %slice_bitcast_fusion.1 = (bf16[96,1,128,64]{2,0,3,1:T(8,128)(2,1)S(1)}, bf16[96,1,128,64]{2,0,3,1:T(8,128)(2,1)S(1)}) fusion(bf16[96,128,64]{1,0,2:T(8,128)(2,1)} %bitcast.76), kind=kLoop, calls=%fused_computation.15 | loop fusion | bytes 4718592 | tf_op jit(solution)/shard_map/stack | solution.py:105
  32.2 0.0 copy-done.6
  32.2 2.4 %maximum_bitcast_fusion = bf16[96,3,128,64,1]{2,0,3,1,4:T(8,128)(2,1)} fusion(bf16[96,1,128,64]{2,0,3,1:T(8,128)(2,1)S(1)} %get-tuple-element.10, bf16[96,1,128,64]{2,0,3,1:T(8,128)(2,1)S(1)} %bitcast.77, bf16[96,1,128,64]{2,0,3,1:T(8,128)(2,1)S(1)} %get-tuple-element.9), kind=kLoop, calls=%fused_computation.3 | loop fusion | flops 4718592 | bytes 9437184 | tf_op jit(solution)/shard_map/stack | solution.py:105
  34.6 0.0 copy-start.4
  34.6 0.0 copy-start.5
  34.6 12.4 %fusion.13.diag_ref = f32[2,64,64]{2,1,0:T(8,128)S(1)} fusion(bf16[2,96,3,128,128]{4,3,2,1,0:T(8,128)(2,1)} %param.7, bf16[96,3,128,64,1]{2,0,3,1,4:T(8,128)(2,1)} %maximum_bitcast_fusion, bf16[12288,64]{0,1:T(8,128)(2,1)S(1)} %copy-done.1), kind=kOutput, calls=%fused_computation.16 | convolution fusion | flops 1410859008 | bytes 25198592 | tf_op jit(solution)/shard_map/bin,rbim->rnm/dot_general | solution.py:109
  47.0 3.4 %all-to-all-done.recv_ref = bf16[32,64,512]{2,1,0:T(8,128)(2,1)} async-done(((bf16[32,64,512]{2,1,0:T(8,128)(2,1)}), bf16[32,64,512]{2,1,0:T(8,128)(2,1)}, u32[]{:S(2)}, u32[]{:S(2)}) %all-to-all-start) | async-done | bytes 2097184 | tf_op jit(solution)/shard_map/all_to_all | solution.py:101
  50.4 0.0 copy-done.4
  50.4 0.0 copy-done.5
  50.4 4.1 %shard_map.65 = f32[2,64,2048]{2,1,0:T(8,128)} custom-call(s32[6]{0:T(128)S(1)} %bitcast.75, s32[32]{0:T(128)S(1)} %copy-done.5, s32[1]{0:T(128)} %bitcast.1.me_ref, bf16[32,64,512]{2,1,0:T(8,128)(2,1)} %all-to-all-done.recv_ref, bf16[6,256,512]{2,1,0:T(8,128)(2,1)S(1)} %bitcast.72, f32[2,64,64]{2,1,0:T(8,128)S(1)} %fusion.13.diag_ref), custom_call_target="tpu_custom_call" | custom-call | tf_op jit(solution)/shard_map/pallas_call | solution.py:116
Async XLA Ops:
  0.0 1.4 %copy-start = (bf16[12288,64]{0,1:T(8,128)(2,1)S(1)}, bf16[12288,64]{0,1:T(8,128)(2,1)}, u32[]{:S(2)}) copy-start(bf16[12288,64]{0,1:T(8,128)(2,1)} %param.6) | copy-start | bytes 4718596
  1.4 0.7 %copy-start.2 = (s32[1,6,512]{2,0,1:T(1,128)S(1)}, s32[1,6,512]{2,0,1:T(1,128)}, u32[]{:S(2)}) copy-start(s32[1,6,512]{2,0,1:T(1,128)} %param.10) | copy-start | bytes 36868
  2.1 0.7 %copy-start.3 = (s32[1,6]{1,0:T(1,128)S(1)}, s32[1,6]{1,0:T(1,128)}, u32[]{:S(2)}) copy-start(s32[1,6]{1,0:T(1,128)} %param.9) | copy-start | bytes 76
  10.1 40.3 %all-to-all-start = ((bf16[32,64,512]{2,1,0:T(8,128)(2,1)}), bf16[32,64,512]{2,1,0:T(8,128)(2,1)}, u32[]{:S(2)}, u32[]{:S(2)}) async-start(bf16[32,64,512]{2,1,0:T(8,128)(2,1)} %get-tuple-element.7), calls=%async_computation | async-start | bytes 4194304 | tf_op jit(solution)/shard_map/all_to_all | solution.py:101
  25.7 1.4 %copy-start.1 = (bf16[12288,64]{0,1:T(8,128)(2,1)S(1)}, bf16[12288,64]{0,1:T(8,128)(2,1)}, u32[]{:S(2)}) copy-start(bf16[12288,64]{0,1:T(8,128)(2,1)} %param.6) | copy-start | bytes 4718596
  28.5 3.6 %copy-start.6 = (bf16[8,8,96,128]{3,2,1,0:T(8,128)(2,1)S(1)}, bf16[8,8,96,128]{3,2,1,0:T(8,128)(2,1)}, u32[]{:S(2)}) copy-start(bf16[8,8,96,128]{3,2,1,0:T(8,128)(2,1)} %copy.17) | copy-start | bytes 4718596
  34.6 15.8 %copy-start.4 = (s32[1,6]{1,0:T(1,128)S(1)}, s32[1,6]{1,0:T(1,128)}, u32[]{:S(2)}) copy-start(s32[1,6]{1,0:T(1,128)} %param.9) | copy-start | bytes 76
  34.6 15.8 %copy-start.5 = (s32[32]{0:T(128)S(1)}, s32[32]{0:T(128)}, u32[]{:S(2)}) copy-start(s32[32]{0:T(128)} %col_ref.1) | copy-start | bytes 388
